TPU v7x, 32 devices: a whole 2x2x4 slice. The times are simulated.
32 devices in a mesh: parts: 2 (over x), sta: 16 (over z, y, core).
Axes of the slice: x: 2, y: 2, z: 4, core: 2. Of those that a mesh axis runs over, the one named last changes fastest.
Arguments:
- raw_traces: bfloat16 [512, 16384], P('parts', 'sta'), parts along dimension 0, may hold values from -6 to 6
- filter_taps: bfloat16 [256], replicated, may hold values from -0.375 to 0.375
- station_order: int32 [512], P('parts'), parts along dimension 0, may hold values from 0 to 255, each once
- window_starts: int32 [32], P('parts'), parts along dimension 0, may hold values from 0 to 2048, as said below
- pairing: int32 [4, 16], replicated, may hold values from 0 to 15, as said below
Outputs:
- correlation: float32 [4, 512, 16, 256], P(None, ('parts', 'sta')), parts along dimension 1
There are 2 independent parts, one for each index of `parts`. A program takes and returns all parts, laid end to end along the dimension named above; an argument that names none is the same for every part. Nothing has to cross between parts.
Inputs may be any that keep to these rules, and one draw needn't show every extreme that they name: Each station appears once; block b holds the stations station_order[b * 16 + j], j < 16. `window_starts`: starts never fall; the first is 0 and the last is 2048; consecutive starts differ by at most 273. Row r is one round of a single round-robin tournament over the 16 blocks: pairing[r, pairing[r, b]] = b, pairing[r, b] != b, and no two rows pair the same two blocks.
All inputs are finite; a program needn't handle non-finite values.
Results may differ from a plain program's by a relative error of at most 0.0049.
Values may be sent and summed in bfloat16 or wider, within the bound.
A program may use at most 128 MiB of HBM per device.

v0:
```python
import math
import jax
import jax.numpy as jnp
from jax import lax
from jax.sharding import PartitionSpec as P

DEC = 4
TAPS = 256
SEG = 2048
BAND = 64
LAGS = 256
ROUNDS = 4
BINS = 1024


def decimate(signal, leading, filter_taps, factor):
    row_count, length = signal.shape
    outputs = length // factor
    per_tile = math.gcd(outputs, 128)
    tile_span = per_tile * factor
    margin = leading.shape[1]
    pieces = 1 + (margin + tile_span - 1) // tile_span
    tile_count = outputs // per_tile
    padded = jnp.concatenate(
        [leading, signal, jnp.zeros((row_count, (pieces - 1) * tile_span - margin), signal.dtype)],
        axis=1,
    )
    tap_count = filter_taps.shape[0]
    positions = jnp.arange(pieces * tile_span, dtype=jnp.int32)[:, None]
    column = jnp.arange(per_tile, dtype=jnp.int32)[None, :]
    tap_index = column * factor + tap_count - 1 - positions
    inside = (tap_index >= 0) & (tap_index < tap_count)
    banded = jnp.where(
        inside,
        jnp.take(filter_taps, jnp.clip(tap_index, 0, tap_count - 1)),
        jnp.zeros((), filter_taps.dtype),
    )
    summed = jnp.zeros((row_count, tile_count, per_tile), jnp.float32)
    for section_index in range(pieces):
        segment = padded[:, section_index * tile_span : section_index * tile_span + length].reshape(
            row_count, tile_count, tile_span
        )
        summed = summed + jnp.einsum(
            "rtu,ui->rti",
            segment,
            banded[section_index * tile_span : (section_index + 1) * tile_span],
            preferred_element_type=jnp.float32,
        )
    return summed.reshape(row_count, outputs)


def dft_matrix(seg_length, bin_count):
    sample = jnp.arange(seg_length, dtype=jnp.int32)
    frequency = jnp.arange(bin_count, dtype=jnp.int32)
    angles = (frequency[:, None] * sample[None, :] % seg_length).astype(jnp.float32) * (
        2.0 * math.pi / seg_length
    )
    taper_curve = 0.5 - 0.5 * jnp.cos(sample.astype(jnp.float32) * (2.0 * math.pi / seg_length))
    joined = jnp.concatenate(
        [jnp.cos(angles) * taper_curve[None, :], -jnp.sin(angles) * taper_curve[None, :]], axis=0
    )
    return joined.astype(jnp.bfloat16)


def lag_matrix(seg_length, bin_count, lag_count, window_count):
    frequency = jnp.arange(bin_count, dtype=jnp.int32)
    lag_offset = jnp.arange(lag_count, dtype=jnp.int32) - lag_count // 2 + seg_length
    angles = (frequency[:, None] * lag_offset[None, :] % seg_length).astype(jnp.float32) * (
        2.0 * math.pi / seg_length
    )
    normalizer = 1.0 / math.sqrt(bin_count * window_count)
    return jnp.stack([jnp.cos(angles) * normalizer, -jnp.sin(angles) * normalizer]).astype(
        jnp.bfloat16
    )


def whiten_flat(spectrum, band_width):
    halves, bin_count, columns = spectrum.shape
    grouped = spectrum.reshape(halves, bin_count // band_width, band_width, columns)
    band_level = jnp.sum(grouped * grouped, axis=(0, 2)) / (2 * band_width)
    scaled = grouped * (1.0 / jnp.sqrt(band_level + 1e-06))[None, :, None]
    return scaled.reshape(spectrum.shape).astype(jnp.bfloat16)


def cross_spectra(left_spec, right_spec):
    turned = jnp.stack([right_spec, jnp.stack([-right_spec[1], right_spec[0]])])
    return jnp.einsum("cfws,kcfwt->kfst", left_spec, turned, preferred_element_type=jnp.float32)


def body(raw_traces, filter_taps, station_order, window_starts, pairing):
    members = lax.axis_size("sta")
    station_count, local_time = raw_traces.shape
    block_size = station_count // members
    margin = TAPS - DEC
    ordered = jnp.take(raw_traces, station_order, axis=0)
    gathered = lax.all_to_all(ordered, "sta", split_axis=0, concat_axis=1, tiled=True)
    leading = jnp.zeros((block_size, margin), gathered.dtype)
    low_rate = decimate(gathered, leading, filter_taps, DEC).astype(jnp.bfloat16)
    window_count = window_starts.shape[0]
    windows = jax.vmap(
        lambda first_sample: lax.dynamic_slice_in_dim(low_rate, first_sample, SEG, 1)
    )(window_starts)
    windows = windows.reshape(window_count * block_size, SEG)
    spectrum = lax.dot_general(
        dft_matrix(SEG, BINS), windows, (((1,), (1,)), ((), ())), preferred_element_type=jnp.float32
    )
    whitened = whiten_flat(spectrum.reshape(2, BINS, window_count * block_size), BAND)
    by_bin = lax.all_to_all(whitened[None], "sta", split_axis=2, concat_axis=0, tiled=True)
    lag_table = lag_matrix(SEG, BINS, LAGS, window_count)
    own_spec = whitened.reshape(2, BINS, window_count, block_size)
    collected = []
    for round_index in range(ROUNDS):
        picked = jnp.take(by_bin, pairing[round_index], axis=0)
        partner_spec = lax.all_to_all(picked, "sta", split_axis=0, concat_axis=2, tiled=True)
        partner_spec = partner_spec.reshape(2, BINS, window_count, block_size)
        cross_spec = cross_spectra(own_spec, partner_spec).astype(jnp.bfloat16)
        collected.append(cross_spec.reshape(2, BINS, block_size * block_size))
    correlated = jnp.einsum(
        "rkfp,kfl->rpl", jnp.stack(collected), lag_table, preferred_element_type=jnp.float32
    )
    return correlated.reshape(ROUNDS, block_size, block_size, LAGS)


def solution(mesh):
    return jax.shard_map(
        body,
        mesh=mesh,
        in_specs=(P("parts", "sta"), P(), P("parts"), P("parts"), P()),
        out_specs=P(None, ("parts", "sta"), None, None),
        check_vma=False,
    )
```

profile of v0, /device:TPU:0, one launch (start us, length us, event | category | flops | bytes accessed | tf_op | source)
XLA Modules:
  0.0 1280.5 jit_solution(12925101330786375420)
XLA Ops:
  3.6 7.4 all-to-all-start
  11.3 35.5 %multiply_convert_fusion.1 = (bf16[1024,2048]{1,0:T(8,128)(2,1)}, bf16[1024,2048]{1,0:T(8,128)(2,1)}) fusion(f32[2048]{0:T(1024)S(1)} %multiply_subtract_fusion), kind=kLoop, calls=%fused_computation.20 | loop fusion | flops 39845888 | bytes 8396800 | tf_op jit(solution)/shard_map/convert.2
  46.8 764.8 %gather_fusion.1 = bf16[131072]{0:T(1024)(128)(2,1)S(1)} fusion(bf16[256]{0:T(256)(128)(2,1)S(1)} %copy-done.2, s32[131072]{0:T(1024)S(1)} %fusion.28), kind=kCustom, calls=%fused_computation.5 | custom fusion | bytes 1048576 | tf_op jit(solution)/shard_map/jit(_take)/gather | solution.py:35
  812.0 8.4 pad_maximum_fusion
  821.7 21.5 %while.1 = (s32[]{:T(128)}, bf16[16,4096]{1,0:T(8,128)(2,1)S(1)}, s32[16,2]{0,1:T(2,128)S(1)}, bf16[16,16,2048]{2,1,0:T(8,128)(2,1)S(1)}, s32[]{:T(128)}) while((s32[]{:T(128)}, bf16[16,4096]{1,0:T(8,128)(2,1)S(1)}, s32[16,2]{0,1:T(2,128)S(1)}, bf16[16,16,2048]{2,1,0:T(8,128)(2,1)S(1)}, s32[]{:T(128)}) %tuple.38), condition=%wide.while_cond, body=%wide.while_body.sunk | while | flops 2 | bytes 131169 | solution.py:101
  843.3 5.8 multiply_reduce_fusion
  849.3 2.1 copy.103
  851.4 6.0 all-to-all-start.1
  857.5 22.9 %all-to-all-done.1 = bf16[1,2,1024,256]{3,1,0,2:T(2,128)(2,1)S(1)} async-done(((bf16[1,2,1024,256]{3,1,0,2:T(2,128)(2,1)}), bf16[1,2,1024,256]{3,1,0,2:T(2,128)(2,1)S(1)}, u32[]{:S(2)}, u32[]{:S(2)}) %all-to-all-start.1) | async-done | bytes 1048608 | tf_op jit(solution)/shard_map/all_to_all | solution.py:108
  882.7 1.6 gather_fusion.2
  884.3 2.3 broadcast_select_fusion.3
  886.7 6.9 all-to-all-start.2
  893.6 1.6 gather_fusion.3
  895.2 2.4 broadcast_select_fusion.2
  897.6 19.0 %all-to-all-done.2 = bf16[16,2,64,256]{3,2,1,0:T(8,128)(2,1)} async-done(((bf16[16,2,64,256]{3,2,1,0:T(8,128)(2,1)}), bf16[16,2,64,256]{3,2,1,0:T(8,128)(2,1)}, u32[]{:S(2)}, u32[]{:S(2)}) %all-to-all-start.2) | async-done | bytes 1048608 | tf_op jit(solution)/shard_map/all_to_all | solution.py:114
  916.6 7.2 all-to-all-start.3
  923.8 1.6 gather_fusion.4
  925.4 2.3 broadcast_select_fusion.1
  927.7 19.0 %all-to-all-done.3 = bf16[16,2,64,256]{3,2,1,0:T(8,128)(2,1)} async-done(((bf16[16,2,64,256]{3,2,1,0:T(8,128)(2,1)}), bf16[16,2,64,256]{3,2,1,0:T(8,128)(2,1)}, u32[]{:S(2)}, u32[]{:S(2)}) %all-to-all-start.3) | async-done | bytes 1048608 | tf_op jit(solution)/shard_map/all_to_all | solution.py:114
  946.8 6.9 all-to-all-start.4
  953.7 1.6 gather_fusion.5
  955.3 2.4 broadcast_select_fusion
  957.6 19.0 %all-to-all-done.4 = bf16[16,2,64,256]{3,2,1,0:T(8,128)(2,1)} async-done(((bf16[16,2,64,256]{3,2,1,0:T(8,128)(2,1)}), bf16[16,2,64,256]{3,2,1,0:T(8,128)(2,1)}, u32[]{:S(2)}, u32[]{:S(2)}) %all-to-all-start.4) | async-done | bytes 1048608 | tf_op jit(solution)/shard_map/all_to_all | solution.py:114
  976.7 6.9 all-to-all-start.5
  983.6 5.5 multiply_convert_fusion.4
  989.0 2.8 copy.109
  991.8 3.2 convert_element_type.96
  995.1 12.1 copy.132
  1007.2 3.8 copy.106
  1011.0 3.8 copy.113
  1014.8 3.8 copy.119
  1019.9 2.3 slice_negate_fusion.2
  1022.2 2.2 slice_negate_fusion.1
  1024.5 2.8 copy.125
  1030.7 4.1 stack_reshape.24
  1036.3 32.0 %copy.110 = bf16[2,2,1024,16,16]{3,4,1,0,2:T(8,128)(2,1)} copy(bf16[2,2,1024,16,16]{2,4,3,1,0:T(8,128)(2,1)S(1)} %pad_maximum_fusion.1) | data formatting | bytes 4194304 | tf_op jit(solution)/shard_map/stack | solution.py:86
  1068.3 13.4 %fusion.6 = bf16[2,1024,16,16]{2,3,0,1:T(8,128)(2,1)} fusion(bf16[2,2,1024,16,16]{3,4,1,0,2:T(8,128)(2,1)} %copy.110, bf16[2,1024,16,16,1]{3,2,0,4,1:T(8,128)(2,1)} %copy.132), kind=kOutput, calls=%fused_computation.24 | convolution fusion | flops 34078720 | bytes 4194304 | tf_op jit(solution)/shard_map/cfws,kcfwt->kfst/dot_general | solution.py:87
  1081.7 10.1 copy.112
  1091.8 2.9 copy.114
  1094.7 2.6 neg.69
  1097.3 2.9 copy.115
  1100.2 2.6 slice.77
  1102.9 2.2 stack_reshape.26
  1107.8 23.2 %copy.116 = bf16[2,2,1024,16,16]{3,4,1,0,2:T(8,128)(2,1)} copy(bf16[2,2,1024,16,16]{2,4,3,1,0:T(8,128)(2,1)S(1)} %pad_maximum_fusion.2) | data formatting | bytes 4194304 | tf_op jit(solution)/shard_map/stack | solution.py:86
  1131.1 13.4 %fusion.7 = bf16[2,1024,16,16]{2,3,0,1:T(8,128)(2,1)} fusion(bf16[2,2,1024,16,16]{3,4,1,0,2:T(8,128)(2,1)} %copy.116, bf16[2,1024,16,16,1]{3,2,0,4,1:T(8,128)(2,1)} %copy.132), kind=kOutput, calls=%fused_computation.25 | convolution fusion | flops 34078720 | bytes 4194304 | tf_op jit(solution)/shard_map/cfws,kcfwt->kfst/dot_general | solution.py:87
  1144.5 10.3 copy.118
  1154.8 2.9 copy.120
  1157.7 2.6 neg.71
  1160.3 2.9 copy.121
  1163.2 2.6 slice.81
  1165.8 2.2 stack_reshape.28
  1169.3 1.4 pad_maximum_fusion.3
  1170.8 23.2 %copy.122 = bf16[2,2,1024,16,16]{3,4,1,0,2:T(8,128)(2,1)} copy(bf16[2,2,1024,16,16]{2,4,3,1,0:T(8,128)(2,1)S(1)} %pad_maximum_fusion.3) | data formatting | bytes 4194304 | tf_op jit(solution)/shard_map/stack | solution.py:86
  1194.0 13.4 %fusion.8 = bf16[2,1024,16,16]{2,3,0,1:T(8,128)(2,1)} fusion(bf16[2,2,1024,16,16]{3,4,1,0,2:T(8,128)(2,1)} %copy.122, bf16[2,1024,16,16,1]{3,2,0,4,1:T(8,128)(2,1)} %copy.132), kind=kOutput, calls=%fused_computation.26 | convolution fusion | flops 34078720 | bytes 4194304 | tf_op jit(solution)/shard_map/cfws,kcfwt->kfst/dot_general | solution.py:87
  1207.4 10.2 copy.124
  1217.6 1.9 copy.126
  1219.4 1.9 neg.73
  1221.4 1.9 copy.127
  1223.2 1.9 slice.85
  1225.2 2.5 stack_reshape.30
  1229.2 23.2 %copy.128 = bf16[2,2,1024,16,16]{3,4,1,0,2:T(8,128)(2,1)} copy(bf16[2,2,1024,16,16]{2,4,3,1,0:T(8,128)(2,1)S(1)} %pad_maximum_fusion.4) | data formatting | bytes 4194304 | tf_op jit(solution)/shard_map/stack | solution.py:86
  1252.5 13.4 %fusion.9 = bf16[2,1024,16,16]{2,3,0,1:T(8,128)(2,1)} fusion(bf16[2,2,1024,16,16]{3,4,1,0,2:T(8,128)(2,1)} %copy.128, bf16[2,1024,16,16,1]{3,2,0,4,1:T(8,128)(2,1)} %copy.132), kind=kOutput, calls=%fused_computation.27 | convolution fusion | flops 34078720 | bytes 4194304 | tf_op jit(solution)/shard_map/cfws,kcfwt->kfst/dot_general | solution.py:87
  1265.9 10.1 copy.130
  1276.1 4.0 fusion.10
  (116 shorter events, 41.2 us)
Async XLA Ops:
  0.0 1.5 copy-start
  0.0 46.8 %copy-start.11 = (s32[16]{0:T(128)S(1)}, s32[16]{0:T(128)}, u32[]{:S(2)}) copy-start(s32[16]{0:T(128)} %param.10) | copy-start | bytes 196
  0.0 46.8 %copy-start.2 = (bf16[256]{0:T(256)(128)(2,1)S(1)}, bf16[256]{0:T(256)(128)(2,1)}, u32[]{:S(2)}) copy-start(bf16[256]{0:T(256)(128)(2,1)} %param.8) | copy-start | bytes 1540
  3.6 816.7 %all-to-all-start = ((bf16[16,16,1024]{2,1,0:T(8,128)(2,1)}), bf16[16,16,1024]{2,1,0:T(8,128)(2,1)S(1)}, u32[]{:S(2)}, u32[]{:S(2)}) async-start(bf16[16,16,1024]{2,1,0:T(8,128)(2,1)} %broadcast_select_fusion.4), calls=%async_computation | async-start | bytes 1048576 | tf_op jit(solution)/shard_map/all_to_all | solution.py:96
  843.3 14.2 %copy-start.10 = (s32[4,16]{1,0:T(4,128)S(1)}, s32[4,16]{1,0:T(4,128)}, u32[]{:S(2)}) copy-start(s32[4,16]{1,0:T(4,128)} %param.11) | copy-start | bytes 772
  851.4 29.0 %all-to-all-start.1 = ((bf16[1,2,1024,256]{3,1,0,2:T(2,128)(2,1)}), bf16[1,2,1024,256]{3,1,0,2:T(2,128)(2,1)S(1)}, u32[]{:S(2)}, u32[]{:S(2)}) async-start(bf16[1,2,1024,256]{3,1,0,2:T(2,128)(2,1)} %copy.103), calls=%async_computation.1 | async-start | bytes 2097152 | tf_op jit(solution)/shard_map/all_to_all | solution.py:108
  880.4 1.0 copy-start.6
  886.7 29.9 %all-to-all-start.2 = ((bf16[16,2,64,256]{3,2,1,0:T(8,128)(2,1)}), bf16[16,2,64,256]{3,2,1,0:T(8,128)(2,1)}, u32[]{:S(2)}, u32[]{:S(2)}) async-start(bf16[16,2,64,256]{3,2,1,0:T(8,128)(2,1)} %broadcast_select_fusion.3), calls=%async_computation.2 | async-start | bytes 2097152 | tf_op jit(solution)/shard_map/all_to_all | solution.py:114
  916.6 30.2 %all-to-all-start.3 = ((bf16[16,2,64,256]{3,2,1,0:T(8,128)(2,1)}), bf16[16,2,64,256]{3,2,1,0:T(8,128)(2,1)}, u32[]{:S(2)}, u32[]{:S(2)}) async-start(bf16[16,2,64,256]{3,2,1,0:T(8,128)(2,1)} %broadcast_select_fusion.2), calls=%async_computation.3 | async-start | bytes 2097152 | tf_op jit(solution)/shard_map/all_to_all | solution.py:114
  946.8 29.9 %all-to-all-start.4 = ((bf16[16,2,64,256]{3,2,1,0:T(8,128)(2,1)}), bf16[16,2,64,256]{3,2,1,0:T(8,128)(2,1)}, u32[]{:S(2)}, u32[]{:S(2)}) async-start(bf16[16,2,64,256]{3,2,1,0:T(8,128)(2,1)} %broadcast_select_fusion.1), calls=%async_computation.4 | async-start | bytes 2097152 | tf_op jit(solution)/shard_map/all_to_all | solution.py:114
  976.7 47.8 %all-to-all-start.5 = ((bf16[16,2,64,256]{3,2,1,0:T(8,128)(2,1)}), bf16[16,2,64,256]{3,2,1,0:T(8,128)(2,1)S(1)}, u32[]{:S(2)}, u32[]{:S(2)}) async-start(bf16[16,2,64,256]{3,2,1,0:T(8,128)(2,1)} %broadcast_select_fusion), calls=%async_computation.5 | async-start | bytes 2097152 | tf_op jit(solution)/shard_map/all_to_all | solution.py:114
  1081.7 21.1 %copy-start.5 = (bf16[1,2,16,64,256]{3,2,4,1,0:T(8,128)(2,1)S(1)}, bf16[1,2,16,64,256]{3,2,4,1,0:T(8,128)(2,1)}, u32[]{:S(2)}) copy-start(bf16[1,2,16,64,256]{3,2,4,1,0:T(8,128)(2,1)} %copy.113) | copy-start | bytes 3145732
  1144.5 21.3 %copy-start.4 = (bf16[1,2,16,64,256]{3,2,4,1,0:T(8,128)(2,1)S(1)}, bf16[1,2,16,64,256]{3,2,4,1,0:T(8,128)(2,1)}, u32[]{:S(2)}) copy-start(bf16[1,2,16,64,256]{3,2,4,1,0:T(8,128)(2,1)} %copy.119) | copy-start | bytes 3145732
  1207.4 17.8 %copy-start.3 = (bf16[1,2,16,64,256]{3,2,4,1,0:T(8,128)(2,1)S(1)}, bf16[1,2,16,64,256]{3,2,4,1,0:T(8,128)(2,1)}, u32[]{:S(2)}) copy-start(bf16[1,2,16,64,256]{3,2,4,1,0:T(8,128)(2,1)} %copy.125) | copy-start | bytes 3145732
  1265.9 10.1 copy-start.7
  1265.9 10.1 copy-start.8
  1265.9 10.1 copy-start.9
  1276.0 4.0 copy-start.1
where the time goes:
time: 1290 us; the launch traced here: 1280 us
  local copies, waits for them, and re-layouts  1020 us (79%)
  waiting for transfers between devices  80 us (6%)
  other arithmetic  76.3 us (6%)
  matrix products  64.1 us (5%)
  starting transfers between devices  41.3 us (3%)
    gather x1, local copies, waits for them, and re-layouts, decimate(): jnp.take(filter_taps, jnp.clip(tap_index, 0, tap_count - 1))  765 us
    another operation x8, local copies, waits for them, and re-layouts, cross_spectra(): turned = jnp.stack([right_spec, jnp.stack([-right_spec[1], right_spec[0]])])  113 us
    all_to_all x4, waiting for transfers between devices, body(): lax.all_to_all(picked, 'sta', split_axis=0, concat_axis=2, tiled=True)  57.1 us
    dot_general x4, matrix products, cross_spectra(): jnp.einsum('cfws,kcfwt->kfst', left_spec, turned, preferred_element_type=...  53.7 us
    another operation x2, other arithmetic  41 us
    convert_element_type x4, local copies, waits for them, and re-layouts, body(): cross_spec = cross_spectra(own_spec, partner_spec).astype(jnp.bfloat16)  40.7 us
    all_to_all x4, starting transfers between devices, body(): lax.all_to_all(picked, 'sta', split_axis=0, concat_axis=2, tiled=True)  27.9 us
  transfers between devices with their start and end apart: 6, of which 4 were waited for; matrix products, arithmetic and copies ran while one was open for 67% of the time, Pallas kernels for 0%

commit v1 on v0

--- a/solution.py
+++ b/solution.py
@@ -11,6 +11,18 @@
 LAGS = 256
 ROUNDS = 4
 BINS = 1024
+
+
+def split_up(x, dim, devices):
+    lengths = x.shape
+    pieces = x.reshape(*lengths[:dim], devices, lengths[dim] // devices, *lengths[dim + 1 :])
+    return jnp.moveaxis(pieces, dim, 0)
+
+
+def laid_out(blocks, dim):
+    shape = list(blocks.shape[1:])
+    shape[dim] *= blocks.shape[0]
+    return jnp.moveaxis(blocks, 0, dim).reshape(shape)
 
 
 def decimate(signal, leading, filter_taps, factor):
@@ -105,7 +117,14 @@
         dft_matrix(SEG, BINS), windows, (((1,), (1,)), ((), ())), preferred_element_type=jnp.float32
     )
     whitened = whiten_flat(spectrum.reshape(2, BINS, window_count * block_size), BAND)
-    by_bin = lax.all_to_all(whitened[None], "sta", split_axis=2, concat_axis=0, tiled=True)
+    size, position = (lax.axis_size("sta"), lax.axis_index("sta"))
+    tiles = split_up(whitened[None], 2, size)
+    outs = [tiles[position]]
+    for step in range(1, size):
+        sent = tiles[(position + step) % size]
+        outs.append(lax.ppermute(sent, "sta", [(i, (i + step) % size) for i in range(size)]))
+    tiles = jnp.stack(outs)[(position - jnp.arange(size)) % size]
+    by_bin = laid_out(tiles, 0)
     lag_table = lag_matrix(SEG, BINS, LAGS, window_count)
     own_spec = whitened.reshape(2, BINS, window_count, block_size)
     collected = []

time: 1290 us -> 1300 us (level)
  waiting for transfers between devices: 80 us -> 66.7 us
    all_to_all x1 -> x0, waiting for transfers between devices: 22.9 us -> none  [body(): lax.all_to_all(whitened[None], 'sta', split_axis=2, concat_axis=0, tiled=...]
    ppermute x0 -> x15, starting transfers between devices: none -> 19.8 us  [body(): lax.ppermute(sent, 'sta', [(i, (i + step) % size) for i in range(size)])]
    gather x48 -> x49, local copies, waits for them, and re-layouts: 21.2 us -> 33 us
  transfers between devices with their start and end apart: 6 -> 20, of which waited for: 4 -> 7; matrix products, arithmetic and copies ran while one was open for 67% -> 67% of each run, Pallas kernels for 0% -> 0%
where the time goes in v1:
time: 1300 us; the launch traced here: 1290 us
  local copies, waits for them, and re-layouts  1030 us (79%)
  other arithmetic  77.1 us (6%)
  waiting for transfers between devices  66.7 us (5%)
  matrix products  64.4 us (5%)
  starting transfers between devices  53.9 us (4%)
    gather x1, local copies, waits for them, and re-layouts, decimate(): jnp.take(filter_taps, jnp.clip(tap_index, 0, tap_count - 1))  765 us
    another operation x8, local copies, waits for them, and re-layouts, cross_spectra(): turned = jnp.stack([right_spec, jnp.stack([-right_spec[1], right_spec[0]])])  113 us
    all_to_all x4, waiting for transfers between devices, body(): lax.all_to_all(picked, 'sta', split_axis=0, concat_axis=2, tiled=True)  57.1 us
    dot_general x4, matrix products, cross_spectra(): jnp.einsum('cfws,kcfwt->kfst', left_spec, turned, preferred_element_type=...  53.7 us
    another operation x2, other arithmetic  40.9 us
    convert_element_type x4, local copies, waits for them, and re-layouts, body(): cross_spec = cross_spectra(own_spec, partner_spec).astype(jnp.bfloat16)  40.6 us
    gather x48, local copies, waits for them, and re-layouts  31.2 us
    all_to_all x4, starting transfers between devices, body(): lax.all_to_all(picked, 'sta', split_axis=0, concat_axis=2, tiled=True)  26.7 us
  transfers between devices with their start and end apart: 20, of which 7 were waited for; matrix products, arithmetic and copies ran while one was open for 67% of the time, Pallas kernels for 0%

profile of v1, /device:TPU:0, one launch (start us, length us, event | category | flops | bytes accessed | tf_op | source)
XLA Modules:
  0.0 1289.5 jit_solution(5398070227189518521)
XLA Ops:
  3.6 7.4 all-to-all-start
  12.2 35.5 %multiply_convert_fusion.1 = (bf16[1024,2048]{1,0:T(8,128)(2,1)}, bf16[1024,2048]{1,0:T(8,128)(2,1)}) fusion(f32[2048]{0:T(1024)S(1)} %multiply_subtract_fusion), kind=kLoop, calls=%fused_computation.21 | loop fusion | flops 39845888 | bytes 8396800 | tf_op jit(solution)/shard_map/convert.2
  47.8 764.8 %gather_fusion.1 = bf16[131072]{0:T(1024)(128)(2,1)S(1)} fusion(bf16[256]{0:T(256)(128)(2,1)S(1)} %copy-done.2, s32[131072]{0:T(1024)S(1)} %fusion.28), kind=kCustom, calls=%fused_computation.5 | custom fusion | bytes 1048576 | tf_op jit(solution)/shard_map/jit(_take)/gather | solution.py:47
  812.9 8.4 pad_maximum_fusion
  822.7 31.2 %while.1 = (s32[]{:T(128)}, bf16[16,4096]{1,0:T(8,128)(2,1)S(1)}, s32[16,2]{0,1:T(2,128)S(1)}, bf16[16,16,2048]{2,1,0:T(8,128)(2,1)}, s32[]{:T(128)}) while((s32[]{:T(128)}, bf16[16,4096]{1,0:T(8,128)(2,1)S(1)}, s32[16,2]{0,1:T(2,128)S(1)}, bf16[16,16,2048]{2,1,0:T(8,128)(2,1)}, s32[]{:T(128)}) %tuple.52), condition=%wide.while_cond, body=%wide.while_body.sunk | while | flops 2 | bytes 132185 | solution.py:113
  853.9 6.1 multiply_reduce_fusion
  860.8 1.7 collective-permute-start.1
  862.4 2.2 collective-permute-start.2
  867.8 4.0 collective-permute-start.6
  872.8 6.5 collective-permute-done.4
  879.9 3.1 collective-permute-start.11
  883.9 2.7 collective-permute-start.13
  887.9 2.2 collective-permute-done.13
  891.1 1.8 gather_fusion.2
  894.5 2.4 broadcast_select_fusion.3
  896.9 6.0 all-to-all-start.1
  904.5 2.4 broadcast_select_fusion.2
  906.9 19.0 %all-to-all-done.1 = bf16[16,2,64,256]{3,2,1,0:T(8,128)(2,1)} async-done(((bf16[16,2,64,256]{3,2,1,0:T(8,128)(2,1)}), bf16[16,2,64,256]{3,2,1,0:T(8,128)(2,1)}, u32[]{:S(2)}, u32[]{:S(2)}) %all-to-all-start.1) | async-done | bytes 1048608 | tf_op jit(solution)/shard_map/all_to_all | solution.py:133
  925.9 6.9 all-to-all-start.2
  934.4 2.4 broadcast_select_fusion.1
  936.8 19.0 %all-to-all-done.2 = bf16[16,2,64,256]{3,2,1,0:T(8,128)(2,1)} async-done(((bf16[16,2,64,256]{3,2,1,0:T(8,128)(2,1)}), bf16[16,2,64,256]{3,2,1,0:T(8,128)(2,1)}, u32[]{:S(2)}, u32[]{:S(2)}) %all-to-all-start.2) | async-done | bytes 1048608 | tf_op jit(solution)/shard_map/all_to_all | solution.py:133
  955.8 6.9 all-to-all-start.3
  964.3 2.4 broadcast_select_fusion
  966.7 19.0 %all-to-all-done.3 = bf16[16,2,64,256]{3,2,1,0:T(8,128)(2,1)} async-done(((bf16[16,2,64,256]{3,2,1,0:T(8,128)(2,1)}), bf16[16,2,64,256]{3,2,1,0:T(8,128)(2,1)}, u32[]{:S(2)}, u32[]{:S(2)}) %all-to-all-start.3) | async-done | bytes 1048608 | tf_op jit(solution)/shard_map/all_to_all | solution.py:133
  985.7 6.9 all-to-all-start.4
  992.6 5.5 multiply_convert_fusion.4
  998.1 2.8 copy.71
  1000.9 3.2 convert_element_type.87
  1004.2 12.1 copy.94
  1016.2 3.8 copy.68
  1020.0 3.8 copy.75
  1023.9 3.8 copy.81
  1029.0 2.3 slice_negate_fusion.2
  1031.2 2.3 slice_negate_fusion.1
  1033.6 2.9 copy.87
  1039.8 4.1 stack_reshape.24
  1045.4 32.0 %copy.72 = bf16[2,2,1024,16,16]{3,4,1,0,2:T(8,128)(2,1)} copy(bf16[2,2,1024,16,16]{2,4,3,1,0:T(8,128)(2,1)S(1)} %pad_maximum_fusion.1) | data formatting | bytes 4194304 | tf_op jit(solution)/shard_map/stack | solution.py:98
  1077.4 13.4 %fusion.6 = bf16[2,1024,16,16]{2,3,0,1:T(8,128)(2,1)} fusion(bf16[2,2,1024,16,16]{3,4,1,0,2:T(8,128)(2,1)} %copy.72, bf16[2,1024,16,16,1]{3,2,0,4,1:T(8,128)(2,1)} %copy.94), kind=kOutput, calls=%fused_computation.25 | convolution fusion | flops 34078720 | bytes 4194304 | tf_op jit(solution)/shard_map/cfws,kcfwt->kfst/dot_general | solution.py:99
  1090.8 10.1 copy.74
  1100.9 2.9 copy.76
  1103.8 2.6 neg.69
  1106.4 2.9 copy.77
  1109.3 2.6 slice.77
  1112.0 2.2 stack_reshape.26
  1116.9 23.2 %copy.78 = bf16[2,2,1024,16,16]{3,4,1,0,2:T(8,128)(2,1)} copy(bf16[2,2,1024,16,16]{2,4,3,1,0:T(8,128)(2,1)S(1)} %pad_maximum_fusion.2) | data formatting | bytes 4194304 | tf_op jit(solution)/shard_map/stack | solution.py:98
  1140.2 13.4 %fusion.7 = bf16[2,1024,16,16]{2,3,0,1:T(8,128)(2,1)} fusion(bf16[2,2,1024,16,16]{3,4,1,0,2:T(8,128)(2,1)} %copy.78, bf16[2,1024,16,16,1]{3,2,0,4,1:T(8,128)(2,1)} %copy.94), kind=kOutput, calls=%fused_computation.26 | convolution fusion | flops 34078720 | bytes 4194304 | tf_op jit(solution)/shard_map/cfws,kcfwt->kfst/dot_general | solution.py:99
  1153.6 10.3 copy.80
  1163.9 2.9 copy.82
  1166.8 2.6 neg.71
  1169.4 2.9 copy.83
  1172.3 2.6 slice.81
  1174.9 2.2 stack_reshape.28
  1179.9 23.2 %copy.84 = bf16[2,2,1024,16,16]{3,4,1,0,2:T(8,128)(2,1)} copy(bf16[2,2,1024,16,16]{2,4,3,1,0:T(8,128)(2,1)S(1)} %pad_maximum_fusion.3) | data formatting | bytes 4194304 | tf_op jit(solution)/shard_map/stack | solution.py:98
  1203.1 13.4 %fusion.8 = bf16[2,1024,16,16]{2,3,0,1:T(8,128)(2,1)} fusion(bf16[2,2,1024,16,16]{3,4,1,0,2:T(8,128)(2,1)} %copy.84, bf16[2,1024,16,16,1]{3,2,0,4,1:T(8,128)(2,1)} %copy.94), kind=kOutput, calls=%fused_computation.27 | convolution fusion | flops 34078720 | bytes 4194304 | tf_op jit(solution)/shard_map/cfws,kcfwt->kfst/dot_general | solution.py:99
  1216.5 10.1 copy.86
  1226.7 1.9 copy.88
  1228.5 1.9 neg.73
  1230.5 1.9 copy.89
  1232.3 1.9 slice.85
  1234.3 2.5 stack_reshape.30
  1238.3 23.2 %copy.90 = bf16[2,2,1024,16,16]{3,4,1,0,2:T(8,128)(2,1)} copy(bf16[2,2,1024,16,16]{2,4,3,1,0:T(8,128)(2,1)S(1)} %pad_maximum_fusion.4) | data formatting | bytes 4194304 | tf_op jit(solution)/shard_map/stack | solution.py:98
  1261.6 13.4 %fusion.9 = bf16[2,1024,16,16]{2,3,0,1:T(8,128)(2,1)} fusion(bf16[2,2,1024,16,16]{3,4,1,0,2:T(8,128)(2,1)} %copy.90, bf16[2,1024,16,16,1]{3,2,0,4,1:T(8,128)(2,1)} %copy.94), kind=kOutput, calls=%fused_computation.28 | convolution fusion | flops 34078720 | bytes 4194304 | tf_op jit(solution)/shard_map/cfws,kcfwt->kfst/dot_general | solution.py:99
  1275.0 10.1 copy.92
  1285.1 4.0 fusion.10
  (160 shorter events, 65.5 us)
Async XLA Ops:
  0.0 1.5 copy-start
  0.0 47.7 %copy-start.10 = (s32[4,16]{1,0:T(4,128)S(1)}, s32[4,16]{1,0:T(4,128)}, u32[]{:S(2)}) copy-start(s32[4,16]{1,0:T(4,128)} %param.11) | copy-start | bytes 772
  0.0 47.8 %copy-start.2 = (bf16[256]{0:T(256)(128)(2,1)S(1)}, bf16[256]{0:T(256)(128)(2,1)}, u32[]{:S(2)}) copy-start(bf16[256]{0:T(256)(128)(2,1)} %param.8) | copy-start | bytes 1540
  3.6 817.7 %all-to-all-start = ((bf16[16,16,1024]{2,1,0:T(8,128)(2,1)}), bf16[16,16,1024]{2,1,0:T(8,128)(2,1)S(1)}, u32[]{:S(2)}, u32[]{:S(2)}) async-start(bf16[16,16,1024]{2,1,0:T(8,128)(2,1)} %broadcast_select_fusion.4), calls=%async_computation | async-start | bytes 1048576 | tf_op jit(solution)/shard_map/all_to_all | solution.py:108
  860.5 6.4 collective-permute-start
  860.8 7.1 collective-permute-start.1
  862.4 9.5 collective-permute-start.2
  864.6 7.9 collective-permute-start.3
  866.1 13.2 %collective-permute-start.4 = (bf16[1,2,64,256]{3,2,1,0:T(8,128)(2,1)S(1)}, bf16[1,2,64,256]{3,2,1,0:T(8,128)(2,1)S(1)}, u32[]{:S(2)}, u32[]{:S(2)}) collective-permute-start(bf16[1,2,64,256]{3,2,1,0:T(8,128)(2,1)S(1)} %get-tuple-element.48), channel_id=1, source_target_pairs={{0,5},{1,6},{2,7},{3,8},{4,9},{5,10},{6,11},{7,12},{8,13},{9,14},{... | collective-permute-start | bytes 196616 | tf_op jit(solution)/shard_map/ppermute | solution.py:125
  866.9 12.6 collective-permute-start.5
  867.8 12.1 collective-permute-start.6
  871.9 11.2 collective-permute-start.7
  872.5 11.4 collective-permute-start.8
  879.3 7.3 collective-permute-start.9
  879.5 8.3 collective-permute-start.10
  879.9 7.9 collective-permute-start.11
  883.0 4.9 collective-permute-start.12
  883.9 6.2 collective-permute-start.13
  886.6 3.5 collective-permute-start.14
  890.1 1.0 copy-start.6
  896.9 29.0 %all-to-all-start.1 = ((bf16[16,2,64,256]{3,2,1,0:T(8,128)(2,1)}), bf16[16,2,64,256]{3,2,1,0:T(8,128)(2,1)}, u32[]{:S(2)}, u32[]{:S(2)}) async-start(bf16[16,2,64,256]{3,2,1,0:T(8,128)(2,1)} %broadcast_select_fusion.3), calls=%async_computation.1 | async-start | bytes 2097152 | tf_op jit(solution)/shard_map/all_to_all | solution.py:133
  925.9 29.9 %all-to-all-start.2 = ((bf16[16,2,64,256]{3,2,1,0:T(8,128)(2,1)}), bf16[16,2,64,256]{3,2,1,0:T(8,128)(2,1)}, u32[]{:S(2)}, u32[]{:S(2)}) async-start(bf16[16,2,64,256]{3,2,1,0:T(8,128)(2,1)} %broadcast_select_fusion.2), calls=%async_computation.2 | async-start | bytes 2097152 | tf_op jit(solution)/shard_map/all_to_all | solution.py:133
  955.8 29.9 %all-to-all-start.3 = ((bf16[16,2,64,256]{3,2,1,0:T(8,128)(2,1)}), bf16[16,2,64,256]{3,2,1,0:T(8,128)(2,1)}, u32[]{:S(2)}, u32[]{:S(2)}) async-start(bf16[16,2,64,256]{3,2,1,0:T(8,128)(2,1)} %broadcast_select_fusion.1), calls=%async_computation.3 | async-start | bytes 2097152 | tf_op jit(solution)/shard_map/all_to_all | solution.py:133
  985.7 47.8 %all-to-all-start.4 = ((bf16[16,2,64,256]{3,2,1,0:T(8,128)(2,1)}), bf16[16,2,64,256]{3,2,1,0:T(8,128)(2,1)S(1)}, u32[]{:S(2)}, u32[]{:S(2)}) async-start(bf16[16,2,64,256]{3,2,1,0:T(8,128)(2,1)} %broadcast_select_fusion), calls=%async_computation.4 | async-start | bytes 2097152 | tf_op jit(solution)/shard_map/all_to_all | solution.py:133
  1090.8 21.1 %copy-start.5 = (bf16[1,2,16,64,256]{3,2,4,1,0:T(8,128)(2,1)S(1)}, bf16[1,2,16,64,256]{3,2,4,1,0:T(8,128)(2,1)}, u32[]{:S(2)}) copy-start(bf16[1,2,16,64,256]{3,2,4,1,0:T(8,128)(2,1)} %copy.75) | copy-start | bytes 3145732
  1153.6 21.3 %copy-start.4 = (bf16[1,2,16,64,256]{3,2,4,1,0:T(8,128)(2,1)S(1)}, bf16[1,2,16,64,256]{3,2,4,1,0:T(8,128)(2,1)}, u32[]{:S(2)}) copy-start(bf16[1,2,16,64,256]{3,2,4,1,0:T(8,128)(2,1)} %copy.81) | copy-start | bytes 3145732
  1216.5 17.7 %copy-start.3 = (bf16[1,2,16,64,256]{3,2,4,1,0:T(8,128)(2,1)S(1)}, bf16[1,2,16,64,256]{3,2,4,1,0:T(8,128)(2,1)}, u32[]{:S(2)}) copy-start(bf16[1,2,16,64,256]{3,2,4,1,0:T(8,128)(2,1)} %copy.87) | copy-start | bytes 3145732
  1275.0 10.1 copy-start.7
  1275.0 10.1 copy-start.8
  1275.0 10.1 copy-start.9
  1285.1 4.0 copy-start.1
